TPU v7x, 128 devices: a whole 4x4x4 slice. The times are simulated.
128 devices in a mesh: chan: 8 (over y, x_lo), blk: 16 (over x_hi, z, core).
Axes of the slice: x: 4 (x_hi: 2, x_lo: 2; x = x_hi * 2 + x_lo), y: 4, z: 4, core: 2. Of those that a mesh axis runs over, the one named last changes fastest.
Arguments:
- voltages: bfloat16 [2, 16, 64, 536576], P(None, 'blk', 'chan'), may hold values from -5.5 to 5.5
- fir_taps: float32 [4, 4096], replicated, may hold values from -3 to 3
- station_flags: int32 [512], replicated, may hold values 0 or 1
- bin_offsets: int32 [256], replicated, may hold values from 0 to 3
Outputs:
- visibilities: bfloat16 [256, 2, 1024, 1024], P('chan', None, 'blk')
All inputs are finite; a program needn't handle non-finite values.
Results may differ from a plain program's by a relative error of at most 0.0034.
Values may be sent and summed in bfloat16 or wider, within the bound.
No kernel may reach another device: no remote copies, remote signals or barrier semaphores. Data moves between devices by JAX's collectives and lax.ppermute only.
A program may use at most 256 MiB of HBM per device.

v0:
```python
import math
import jax
import jax.numpy as jnp
from jax import lax
from jax.sharding import PartitionSpec as P

NFFT = 4096
KEEP = 256
TAPS = 4
FRAMES = 128


def phase_table(length, kept):
    row_index = lax.broadcasted_iota(jnp.int32, (length, kept), 0)
    column_index = lax.broadcasted_iota(jnp.int32, (length, kept), 1)
    phases = row_index * column_index % length
    angles = phases.astype(jnp.float32) * (2.0 * math.pi / length)
    cosine = jnp.cos(angles)
    sine_part = jnp.sin(angles)
    upper = jnp.stack([cosine, -sine_part], axis=1)
    lower = jnp.stack([sine_part, cosine], axis=1)
    return jnp.stack([upper, lower])


def correlate(mine, others):
    rotated = jnp.stack([-others[1], others[0]])
    real_part = jnp.einsum("pcif,pcjf->cij", mine, others, preferred_element_type=jnp.float32)
    imag_part = jnp.einsum("pcif,pcjf->cij", mine, rotated, preferred_element_type=jnp.float32)
    return jnp.stack([real_part, imag_part], axis=1)


def on_device(voltages, fir_taps, station_flags, bin_offsets):
    inputs_here = voltages.shape[2]
    chan_total = lax.axis_size("chan")
    planes = voltages.reshape(2, inputs_here, FRAMES + TAPS - 1, NFFT)
    filtered = jnp.zeros((2, inputs_here, FRAMES, NFFT), jnp.float32)
    for tap_index in range(TAPS):
        filtered = (
            filtered
            + planes[:, :, tap_index : tap_index + FRAMES, :].astype(jnp.float32)
            * fir_taps[tap_index]
        )
    first_input = (
        lax.axis_index("blk") * (inputs_here * chan_total) + lax.axis_index("chan") * inputs_here
    )
    weights = lax.dynamic_slice_in_dim(
        jnp.repeat(station_flags, 2).astype(jnp.float32), first_input, inputs_here, 0
    )
    spectrum = jnp.einsum(
        "pifn,pnqk->qkif",
        filtered,
        phase_table(NFFT, KEEP),
        precision=lax.Precision.HIGHEST,
        preferred_element_type=jnp.float32,
    )
    spectra = (spectrum / math.sqrt(2.0 * NFFT) * weights[:, None]).astype(jnp.bfloat16)
    scales = jnp.exp2(-bin_offsets.astype(jnp.float32)) / FRAMES
    local = lax.all_to_all(spectra, "chan", split_axis=1, concat_axis=2, tiled=True)
    group_channels = local.shape[1]
    sums = correlate(local, lax.all_gather(local, "blk", axis=2, tiled=True))
    first_channel = lax.axis_index("chan") * group_channels
    factor = lax.dynamic_slice_in_dim(scales, first_channel, group_channels, 0)
    return (sums * factor[:, None, None, None]).astype(jnp.bfloat16)


def solution(mesh):
    in_specs = (P(None, "blk", "chan", None), P(), P(), P())
    out_specs = P("chan", None, "blk", None)
    return jax.shard_map(
        on_device, mesh=mesh, in_specs=in_specs, out_specs=out_specs, check_vma=False
    )
```

profile of v0, /device:TPU:1, one launch (start us, length us, event | category | flops | bytes accessed | tf_op | source)
XLA Modules:
  0.0 397.2 jit_solution(11936473295137632323)
XLA Ops:
  6.5 0.0 copy-start.2
  6.5 0.0 copy-start.1
  6.5 0.0 all-gather.2.cloned.1.call-start
  6.5 16.5 %fusion.40 = f32[4096,1,256]{0,2,1:T(8,128)} fusion(), kind=kLoop, calls=%fused_computation.48 | loop fusion | flops 15728640 | bytes 4194304 | tf_op jit(solution)/shard_map/neg | solution.py:20
  23.1 17.6 %fusion.38 = (f32[4096,1,256]{0,2,1:T(8,128)}, f32[4096,1,256]{0,2,1:T(8,128)}) fusion(), kind=kLoop, calls=%fused_computation.46 | loop fusion | flops 14680064 | bytes 8388608 | tf_op jit(solution)/shard_map/sin | solution.py:19
  40.6 0.0 copy-done.2
  40.7 0.0 copy-done.1
  40.7 0.1 broadcast_in_dim.4
  40.9 0.2 convert_element_type.58
  41.0 44.0 %fusion.45 = (bf16[2,8,128,4096]{3,1,2,0:T(8,128)(2,1)}, bf16[2,8,128,4096]{3,1,2,0:T(8,128)(2,1)}, bf16[2,8,128,4096]{3,1,2,0:T(8,128)(2,1)}, bf16[2,8,128,4096]{3,1,2,0:T(8,128)(2,1)}) fusion(bf16[2,8,131,4096]{3,1,2,0:T(8,128)(2,1)} %bitcast.53), kind=kLoop, calls=%fused_computation.54 | loop fusion | bytes 134217728 | tf_op jit(solution)/shard_map/slice | solution.py:40
  85.0 0.1 dynamic-slice_multiply_fusion
  85.1 0.0 copy-start
  85.1 13.3 %maximum_bitcast_fusion.2 = (f32[1,4096,2,256]{1,3,0,2:T(8,128)}, f32[1,4096,2,256]{1,3,0,2:T(8,128)}) fusion(f32[4096,1,256]{0,2,1:T(8,128)} %fusion.40, f32[4096,1,256]{0,2,1:T(8,128)} %get-tuple-element.18, f32[4096,1,256]{0,2,1:T(8,128)} %get-tuple-element.17), kind=kLoop, calls=%fused_computation.31 | loop fusion | flops 4194304 | bytes 29360128 | tf_op jit(solution)/shard_map/stack | solution.py:22
  98.5 3.0 copy-done
  101.4 0.0 copy-start.3
  101.4 100.0 %fusion.37 = bf16[2,256,8,128]{3,1,2,0:T(8,128)(2,1)S(1)} fusion(bf16[2,8,128,4096]{3,1,2,0:T(8,128)(2,1)} %get-tuple-element.8, bf16[2,8,128,4096]{3,1,2,0:T(8,128)(2,1)} %get-tuple-element.6, bf16[2,8,128,4096]{3,1,2,0:T(8,128)(2,1)} %get-tuple-element.7, bf16[2,8,128,4096]{3,1,2,0:T(8,128)(2,1)S(1)} %copy-done, f32[4096]{0:T(1024)S(1)} %bitcast.60, ...), kind=kOutput, calls=%fused_computation.45 | convolution fusion | flops 51637125120 | bytes 85000224 | tf_op jit(solution)/shard_map/pifn,pnqk->qkif/dot_general | solution.py:49
  201.4 0.7 copy.24
  202.1 20.7 %all_to_all.18 = bf16[2,256,8,128]{3,2,0,1:T(8,128)(2,1)S(1)} all-to-all(bf16[2,256,8,128]{3,2,0,1:T(8,128)(2,1)S(1)} %copy.24), channel_id=1, replica_groups=mesh['chan'=8,'blk'=16] {'chan'}, dimensions={1} | all-to-all | bytes 2097152 | tf_op jit(solution)/shard_map/all_to_all | solution.py:58
  222.8 1.3 copy.74
  224.0 0.0 all-gather.2.cloned.1.call-update
  224.1 0.0 copy-done.3
  224.1 0.1 dynamic_slice.7
  224.2 111.1 %all-gather.2.cloned.1.call-done = bf16[2,32,1024,128]{3,2,0,1:T(8,128)(2,1)} async-done(((bf16[2,32,64,128]{3,2,0,1:T(8,128)(2,1)}), bf16[2,32,1024,128]{3,2,0,1:T(8,128)(2,1)}) %all-gather.2.cloned.1.call-update) | async-done | bytes 16777232 | tf_op jit(solution)/shard_map/all_gather | solution.py:60
  335.2 11.7 %slice_negate_fusion = (bf16[1,32,1024,128]{3,2,0,1:T(8,128)(2,1)}, bf16[1,32,1024,128]{3,2,0,1:T(8,128)(2,1)}) fusion(bf16[2,32,1024,128]{3,2,0,1:T(8,128)(2,1)} %all-gather.2.cloned.1.call-done), kind=kLoop, calls=%fused_computation.30 | loop fusion | flops 4194304 | bytes 33554432 | tf_op jit(solution)/shard_map/neg | solution.py:26
  346.9 10.7 %fusion.34 = f32[32,1,64,1024]{3,2,0,1:T(8,128)} fusion(bf16[1,32,1024,128]{3,2,0,1:T(8,128)(2,1)} %get-tuple-element.10, bf16[1,32,1024,128]{3,2,0,1:T(8,128)(2,1)} %get-tuple-element.9, bf16[2,8,32,8,128]{4,3,0,2,1:T(8,128)(2,1)S(1)} %bitcast.55), kind=kOutput, calls=%fused_computation.43 | convolution fusion | flops 1082130432 | bytes 26214400 | tf_op jit(solution)/shard_map/pcif,pcjf->cij/dot_general | solution.py:28
  357.6 14.3 %convolution_bitcast_fusion = f32[32,1,64,1024]{3,2,0,1:T(8,128)} fusion(bf16[2,32,1024,128]{3,2,0,1:T(8,128)(2,1)} %all-gather.2.cloned.1.call-done, bf16[2,8,32,8,128]{4,3,0,2,1:T(8,128)(2,1)S(1)} %bitcast.56), kind=kOutput, calls=%fused_computation.42 | convolution fusion | flops 1073741824 | bytes 26214400 | tf_op jit(solution)/shard_map/pcif,pcjf->cij/dot_general | solution.py:27
  371.9 9.8 %fusion.19 = bf16[32,2,64,1024]{3,2,0,1:T(8,128)(2,1)} fusion(f32[32,1,64,1024]{3,2,0,1:T(8,128)} %fusion.34, f32[32,1,64,1024]{3,2,0,1:T(8,128)} %convolution_bitcast_fusion, f32[32]{0:T(128)S(1)} %dynamic_slice.7), kind=kLoop, calls=%fused_computation.21 | loop fusion | flops 12582912 | bytes 25165952 | tf_op jit(solution)/shard_map/convert_element_type | solution.py:63
  381.8 8.6 %copy.26 = bf16[32,2,64,1024]{3,2,1,0:T(8,128)(2,1)} copy(bf16[32,2,64,1024]{3,2,0,1:T(8,128)(2,1)} %fusion.19) | data formatting | bytes 16777216 | tf_op jit(solution)/shard_map/convert_element_type | solution.py:63
  (3 shorter events, 0.1 us)
Async XLA Ops:
  6.5 34.1 %copy-start.2 = (s32[512]{0:T(512)S(1)}, s32[512]{0:T(512)}, u32[]{:S(2)}) copy-start(s32[512]{0:T(512)} %param.6) | copy-start | bytes 6148
  6.5 34.1 %copy-start.1 = (f32[4,4096]{1,0:T(4,128)S(1)}, f32[4,4096]{1,0:T(4,128)}, u32[]{:S(2)}) copy-start(f32[4,4096]{1,0:T(4,128)} %param.5) | copy-start | bytes 196612
  6.5 328.7 %all-gather.2.cloned.1.call-start = ((), (), s32[]{:S(2)}) async-start(), calls=%async_computation.1 | async-start | bytes 17825792 | tf_op jit(solution)/shard_map/all_gather | solution.py:60
  85.1 16.3 %copy-start = (bf16[2,8,128,4096]{3,1,2,0:T(8,128)(2,1)S(1)}, bf16[2,8,128,4096]{3,1,2,0:T(8,128)(2,1)}, u32[]{:S(2)}) copy-start(bf16[2,8,128,4096]{3,1,2,0:T(8,128)(2,1)} %get-tuple-element.5) | copy-start | bytes 50331652
  101.4 122.6 %copy-start.3 = (s32[256]{0:T(256)S(1)}, s32[256]{0:T(256)}, u32[]{:S(2)}) copy-start(s32[256]{0:T(256)} %param.7) | copy-start | bytes 3076
Sparse Core Ops, SparseCore 0:
  224.2 110.9 all-gather.1
where the time goes:
time: 397 us
  matrix products  125 us (31%)
  waiting for transfers between devices  111 us (28%)
  other arithmetic  69 us (17%)
  local copies, waits for them, and re-layouts  57.9 us (15%)
  blocking collectives  20.7 us (5%)
  between operations  13.5 us (3%)
    all_gather x1, waiting for transfers between devices, on_device(): sums = correlate(local, lax.all_gather(local, 'blk', axis=2, tiled=True))  111 us
    dot_general x1, matrix products, on_device(): jnp.einsum('pifn,pnqk->qkif', filtered, phase_table(NFFT, KEEP), precisio...  100 us
    slice x1, local copies, waits for them, and re-layouts, on_device(): planes[:, :, tap_index:tap_index + FRAMES, :].astype(jnp.float32)  44 us
    all_to_all x1, blocking collectives, on_device(): lax.all_to_all(spectra, 'chan', split_axis=1, concat_axis=2, tiled=True)  20.7 us
    sin x1, other arithmetic, phase_table(): sine_part = jnp.sin(angles)  17.6 us
    neg x1, other arithmetic, phase_table(): upper = jnp.stack([cosine, -sine_part], axis=1)  16.5 us
    dot_general x1, matrix products, correlate(): jnp.einsum('pcif,pcjf->cij', mine, others, preferred_element_type=jnp.flo...  14.3 us
    another operation x1, other arithmetic, phase_table(): return jnp.stack([upper, lower])  13.3 us
  transfers between devices with their start and end apart: 1, of which 1 were waited for; matrix products, arithmetic and copies ran while one was open for 0% of the time, Pallas kernels for 0%

commit v1 on v0

--- a/solution.py
+++ b/solution.py
@@ -57,7 +57,12 @@
     scales = jnp.exp2(-bin_offsets.astype(jnp.float32)) / FRAMES
     local = lax.all_to_all(spectra, "chan", split_axis=1, concat_axis=2, tiled=True)
     group_channels = local.shape[1]
-    sums = correlate(local, lax.all_gather(local, "blk", axis=2, tiled=True))
+    sums = correlate(
+        local,
+        jnp.concatenate(
+            lax.all_to_all(jnp.stack([local] * lax.axis_size("blk")), "blk", 0, 0), axis=2
+        ),
+    )
     first_channel = lax.axis_index("chan") * group_channels
     factor = lax.dynamic_slice_in_dim(scales, first_channel, group_channels, 0)
     return (sums * factor[:, None, None, None]).astype(jnp.bfloat16)

time: 397 us -> 579 us (1.46)
  waiting for transfers between devices: 111 us -> 254 us
  local copies, waits for them, and re-layouts: 57.9 us -> 96.7 us
  between operations: 13.5 us -> 0.09 us
  starting transfers between devices: 0.01 us -> 9.49 us
    all_to_all x0 -> x1, waiting for transfers between devices: none -> 254 us  [on_device(): lax.all_to_all(jnp.stack([local] * lax.axis_size('blk')), 'blk', 0, 0)]
    all_gather x1 -> x0, waiting for transfers between devices: 111 us -> none  [on_device(): sums = correlate(local, lax.all_gather(local, 'blk', axis=2, tiled=True))]
    reshape x0 -> x1, local copies, waits for them, and re-layouts: none -> 14 us  [on_device(): jnp.concatenate(lax.all_to_all(jnp.stack([local] * lax.axis_size('blk')),...]
    slice x0 -> x1, local copies, waits for them, and re-layouts: none -> 9.92 us  [correlate(): rotated = jnp.stack([-others[1], others[0]])]
    neg x0 -> x1, local copies, waits for them, and re-layouts: none -> 9.6 us  [correlate(): rotated = jnp.stack([-others[1], others[0]])]
    all_to_all x0 -> x1, starting transfers between devices: none -> 9.49 us  [on_device(): lax.all_to_all(jnp.stack([local] * lax.axis_size('blk')), 'blk', 0, 0)]
    another operation x0 -> x1, local copies, waits for them, and re-layouts: none -> 6.27 us  [on_device(): jnp.stack([local] * lax.axis_size('blk'))]
where the time goes in v1:
time: 579 us; the launch traced here: 573 us
  waiting for transfers between devices  254 us (44%)
  matrix products  125 us (22%)
  local copies, waits for them, and re-layouts  96.7 us (17%)
  other arithmetic  67.3 us (12%)
  blocking collectives  20.7 us (4%)
  starting transfers between devices  9.49 us (2%)
    all_to_all x1, waiting for transfers between devices, on_device(): lax.all_to_all(jnp.stack([local] * lax.axis_size('blk')), 'blk', 0, 0)  254 us
    dot_general x1, matrix products, on_device(): jnp.einsum('pifn,pnqk->qkif', filtered, phase_table(NFFT, KEEP), precisio...  100 us
    slice x1, local copies, waits for them, and re-layouts, on_device(): planes[:, :, tap_index:tap_index + FRAMES, :].astype(jnp.float32)  44 us
    all_to_all x1, blocking collectives, on_device(): lax.all_to_all(spectra, 'chan', split_axis=1, concat_axis=2, tiled=True)  20.7 us
    sin x1, other arithmetic, phase_table(): sine_part = jnp.sin(angles)  17.5 us
    neg x1, other arithmetic, phase_table(): upper = jnp.stack([cosine, -sine_part], axis=1)  16.5 us
    dot_general x1, matrix products, correlate(): jnp.einsum('pcif,pcjf->cij', mine, others, preferred_element_type=jnp.flo...  14.1 us
    reshape x1, local copies, waits for them, and re-layouts, on_device(): jnp.concatenate(lax.all_to_all(jnp.stack([local] * lax.axis_size('blk')),...  14 us
  transfers between devices with their start and end apart: 1, of which 1 were waited for; matrix products, arithmetic and copies ran while one was open for 0% of the time, Pallas kernels for 0%

profile of v1, /device:TPU:1, one launch (start us, length us, event | category | flops | bytes accessed | tf_op | source)
XLA Modules:
  0.0 573.4 jit_solution(1268391405482961371)
XLA Ops:
  0.0 0.0 copy-start.2
  0.0 0.0 copy-start.1
  0.0 16.5 %fusion.40 = f32[4096,1,256]{0,2,1:T(8,128)} fusion(), kind=kLoop, calls=%fused_computation.48 | loop fusion | flops 15728640 | bytes 4194304 | tf_op jit(solution)/shard_map/neg | solution.py:20
  16.5 17.5 %fusion.38 = (f32[4096,1,256]{0,2,1:T(8,128)}, f32[4096,1,256]{0,2,1:T(8,128)}) fusion(), kind=kLoop, calls=%fused_computation.46 | loop fusion | flops 14680064 | bytes 8388608 | tf_op jit(solution)/shard_map/sin | solution.py:19
  34.1 0.0 copy-done.2
  34.1 0.0 copy-done.1
  34.1 0.1 broadcast_in_dim.4
  34.3 0.2 convert_element_type.58
  34.4 44.0 %fusion.45 = (bf16[2,8,128,4096]{3,1,2,0:T(8,128)(2,1)}, bf16[2,8,128,4096]{3,1,2,0:T(8,128)(2,1)}, bf16[2,8,128,4096]{3,1,2,0:T(8,128)(2,1)}, bf16[2,8,128,4096]{3,1,2,0:T(8,128)(2,1)}) fusion(bf16[2,8,131,4096]{3,1,2,0:T(8,128)(2,1)} %bitcast.57), kind=kLoop, calls=%fused_computation.54 | loop fusion | bytes 134217728 | tf_op jit(solution)/shard_map/slice | solution.py:40
  78.5 0.1 dynamic-slice_multiply_fusion
  78.5 0.0 copy-start
  78.6 13.5 %maximum_bitcast_fusion.2 = (f32[1,4096,2,256]{1,3,0,2:T(8,128)}, f32[1,4096,2,256]{1,3,0,2:T(8,128)}) fusion(f32[4096,1,256]{0,2,1:T(8,128)} %fusion.40, f32[4096,1,256]{0,2,1:T(8,128)} %get-tuple-element.18, f32[4096,1,256]{0,2,1:T(8,128)} %get-tuple-element.17), kind=kLoop, calls=%fused_computation.31 | loop fusion | flops 4194304 | bytes 29360128 | tf_op jit(solution)/shard_map/stack | solution.py:22
  92.0 2.9 copy-done
  94.9 100.0 %fusion.37 = bf16[2,256,8,128]{3,1,2,0:T(8,128)(2,1)S(1)} fusion(bf16[2,8,128,4096]{3,1,2,0:T(8,128)(2,1)} %get-tuple-element.8, bf16[2,8,128,4096]{3,1,2,0:T(8,128)(2,1)} %get-tuple-element.6, bf16[2,8,128,4096]{3,1,2,0:T(8,128)(2,1)} %get-tuple-element.7, bf16[2,8,128,4096]{3,1,2,0:T(8,128)(2,1)S(1)} %copy-done, f32[4096]{0:T(1024)S(1)} %bitcast.69, ...), kind=kOutput, calls=%fused_computation.45 | convolution fusion | flops 51637125120 | bytes 85000224 | tf_op jit(solution)/shard_map/pifn,pnqk->qkif/dot_general | solution.py:49
  194.8 0.7 copy.24
  195.5 20.7 %all_to_all.23 = bf16[2,256,8,128]{3,2,0,1:T(8,128)(2,1)S(1)} all-to-all(bf16[2,256,8,128]{3,2,0,1:T(8,128)(2,1)S(1)} %copy.24), channel_id=1, replica_groups=mesh['chan'=8,'blk'=16] {'chan'}, dimensions={1} | all-to-all | bytes 2097152 | tf_op jit(solution)/shard_map/all_to_all | solution.py:58
  216.2 0.3 copy.77
  216.5 6.3 %stack.25 = bf16[16,2,32,64,128]{4,3,1,2,0:T(8,128)(2,1)} broadcast(bf16[2,32,64,128]{3,2,0,1:T(8,128)(2,1)S(1)} %bitcast.66), dimensions={1,2,3,4} | broadcast | bytes 17825792 | tf_op jit(solution)/shard_map/stack | solution.py:63
  222.8 0.0 copy-start.3
  222.8 9.5 %all-to-all-start.1 = ((bf16[16,2,32,64,128]{4,3,1,2,0:T(8,128)(2,1)}), bf16[16,2,32,64,128]{4,3,1,2,0:T(8,128)(2,1)}, u32[]{:S(2)}, u32[]{:S(2)}) async-start(bf16[16,2,32,64,128]{4,3,1,2,0:T(8,128)(2,1)} %stack.25), calls=%async_computation.1 | async-start | bytes 33554432 | tf_op jit(solution)/shard_map/all_to_all | solution.py:63
  232.3 0.0 copy-done.3
  232.3 0.1 dynamic_slice.7
  232.4 254.3 %all-to-all-done.1 = bf16[16,2,32,64,128]{4,3,1,2,0:T(8,128)(2,1)} async-done(((bf16[16,2,32,64,128]{4,3,1,2,0:T(8,128)(2,1)}), bf16[16,2,32,64,128]{4,3,1,2,0:T(8,128)(2,1)}, u32[]{:S(2)}, u32[]{:S(2)}) %all-to-all-start.1) | async-done | bytes 16777248 | tf_op jit(solution)/shard_map/all_to_all | solution.py:63
  486.6 14.0 %copy.26 = bf16[2,32,16,64,128]{4,3,2,0,1:T(8,128)(2,1)} copy(bf16[2,32,16,64,128]{4,3,0,1,2:T(8,128)(2,1)} %bitcast.17) | data formatting | bytes 33554432 | tf_op jit(solution)/shard_map/reshape | solution.py:62
  500.7 11.7 %slice_negate_fusion = (bf16[1,32,16,64,128]{4,3,0,1,2:T(8,128)(2,1)}, bf16[1,32,16,64,128]{4,3,0,1,2:T(8,128)(2,1)}) fusion(bf16[2,32,16,64,128]{4,3,0,1,2:T(8,128)(2,1)} %bitcast.17), kind=kLoop, calls=%fused_computation.30 | loop fusion | flops 4194304 | bytes 33554432 | tf_op jit(solution)/shard_map/neg | solution.py:26
  512.4 14.1 %convolution_bitcast_fusion = f32[32,1,64,1024]{3,2,0,1:T(8,128)} fusion(bf16[2,32,1024,128]{3,2,0,1:T(8,128)(2,1)} %bitcast.58, bf16[2,8,32,8,128]{4,3,0,2,1:T(8,128)(2,1)S(1)} %bitcast.62), kind=kOutput, calls=%fused_computation.42 | convolution fusion | flops 1073741824 | bytes 26214400 | tf_op jit(solution)/shard_map/pcif,pcjf->cij/dot_general | solution.py:27
  526.5 9.6 %copy.27 = bf16[1,32,16,64,128]{4,3,2,1,0:T(8,128)(2,1)} copy(bf16[1,32,16,64,128]{4,3,0,1,2:T(8,128)(2,1)} %get-tuple-element.9) | data formatting | bytes 16777216 | tf_op jit(solution)/shard_map/neg | solution.py:26
  536.1 0.0 slice-start
  536.2 9.9 %copy.28 = bf16[1,32,16,64,128]{4,3,2,1,0:T(8,128)(2,1)} copy(bf16[1,32,16,64,128]{4,3,0,1,2:T(8,128)(2,1)} %get-tuple-element.10) | data formatting | bytes 16777216 | tf_op jit(solution)/shard_map/slice | solution.py:26
  546.1 0.0 slice-start.1
  546.1 10.8 %fusion.34 = f32[32,1,64,1024]{3,2,0,1:T(8,128)} fusion(bf16[1,32,1024,128]{3,2,0,1:T(8,128)(2,1)} %bitcast.65, bf16[1,32,1024,128]{3,2,0,1:T(8,128)(2,1)} %bitcast.64, bf16[2,8,32,8,128]{4,3,0,2,1:T(8,128)(2,1)S(1)} %bitcast.63), kind=kOutput, calls=%fused_computation.43 | convolution fusion | flops 1082130432 | bytes 26214400 | tf_op jit(solution)/shard_map/pcif,pcjf->cij/dot_general | solution.py:28
  556.9 0.0 slice-done
  556.9 0.0 slice-done.1
  556.9 7.9 %fusion.19 = bf16[32,2,64,1024]{3,2,0,1:T(8,128)(2,1)} fusion(f32[32,1,64,1024]{3,2,0,1:T(8,128)} %fusion.34, f32[32,1,64,1024]{3,2,0,1:T(8,128)S(1)} %bitcast.60, f32[32]{0:T(128)S(1)} %dynamic_slice.7), kind=kLoop, calls=%fused_computation.21 | loop fusion | flops 12582912 | bytes 25165952 | tf_op jit(solution)/shard_map/convert_element_type | solution.py:68
  564.9 8.6 %copy.29 = bf16[32,2,64,1024]{3,2,1,0:T(8,128)(2,1)} copy(bf16[32,2,64,1024]{3,2,0,1:T(8,128)(2,1)} %fusion.19) | data formatting | bytes 16777216 | tf_op jit(solution)/shard_map/convert_element_type | solution.py:68
  (4 shorter events, 0.1 us)
Async XLA Ops:
  0.0 34.1 %copy-start.2 = (s32[512]{0:T(512)S(1)}, s32[512]{0:T(512)}, u32[]{:S(2)}) copy-start(s32[512]{0:T(512)} %param.6) | copy-start | bytes 6148
  0.0 34.1 %copy-start.1 = (f32[4,4096]{1,0:T(4,128)S(1)}, f32[4,4096]{1,0:T(4,128)}, u32[]{:S(2)}) copy-start(f32[4,4096]{1,0:T(4,128)} %param.5) | copy-start | bytes 196612
  78.5 16.3 %copy-start = (bf16[2,8,128,4096]{3,1,2,0:T(8,128)(2,1)S(1)}, bf16[2,8,128,4096]{3,1,2,0:T(8,128)(2,1)}, u32[]{:S(2)}) copy-start(bf16[2,8,128,4096]{3,1,2,0:T(8,128)(2,1)} %get-tuple-element.5) | copy-start | bytes 50331652
  222.8 9.5 %copy-start.3 = (s32[256]{0:T(256)S(1)}, s32[256]{0:T(256)}, u32[]{:S(2)}) copy-start(s32[256]{0:T(256)} %param.7) | copy-start | bytes 3076
  222.8 263.9 %all-to-all-start.1 = ((bf16[16,2,32,64,128]{4,3,1,2,0:T(8,128)(2,1)}), bf16[16,2,32,64,128]{4,3,1,2,0:T(8,128)(2,1)}, u32[]{:S(2)}, u32[]{:S(2)}) async-start(bf16[16,2,32,64,128]{4,3,1,2,0:T(8,128)(2,1)} %stack.25), calls=%async_computation.1 | async-start | bytes 33554432 | tf_op jit(solution)/shard_map/all_to_all | solution.py:63
  536.1 20.8 %slice-start = ((s8[8388608]{0:T(1024)(128)(4,1)}), s8[4194304]{0:T(1024)(128)(4,1)S(1)}, s32[]{:S(2)}) async-start(s8[8388608]{0:T(1024)(128)(4,1)} %bitcast.59), calls=%async_computation.2 | async-start | bytes 8388608
  546.1 10.8 %slice-start.1 = ((s8[8388608]{0:T(1024)(128)(4,1)}), s8[4194304]{0:T(1024)(128)(4,1)S(1)}, s32[]{:S(2)}) async-start(s8[8388608]{0:T(1024)(128)(4,1)} %bitcast.59), calls=%async_computation.3 | async-start | bytes 8388608
